TPU v7x, 256 devices: a whole 4x4x8 slice. The times are simulated.
256 devices in a mesh: prompt: 16 (over y_lo, z), slab: 16 (over y_hi, x, core).
Axes of the slice: x: 4, y: 4 (y_hi: 2, y_lo: 2; y = y_hi * 2 + y_lo), z: 8, core: 2. Of those that a mesh axis runs over, the one named last changes fastest.
Arguments:
- queries: bfloat16 [16, 8192, 1536], P('prompt', 'slab'), may hold values from -8 to 8
- key_value: bfloat16 [2, 16, 8192, 1536], P(None, 'prompt', 'slab'), may hold values from -6 to 6
- text_kv: bfloat16 [2, 16, 256, 1536], P(None, 'prompt', 'slab'), may hold values from -9 to 9
- residual: bfloat16 [16, 8192, 3072], P('prompt', 'slab'), may hold values from -1.5 to 1.5
- gate: float32 [16, 3072], P('prompt'), may hold values from 0.5 to 2
- bias: float32 [3072], replicated, may hold values from -1.2 to 1.2
- proj_weight: bfloat16 [1536, 3072], P('prompt'), may hold values from -0.15625 to 0.15625
- block_list: int32 [64, 8], P('slab'), may hold values from 0 to 63, as said below
- block_count: int32 [64], P('slab'), may hold values from 2 to 8, as said below
Outputs:
- output: bfloat16 [16, 8192, 3072], P('prompt', 'slab')
Inputs may be any that keep to these rules, and one draw needn't show every extreme that they name: `block_list`: entry 0 of row t is t itself; entries 1 to block_count[t] - 1 are distinct tiles other than t that lie in the slab of t or in one of the two slabs beside it (tile g lies in slab g // 4); the remaining entries repeat t. `block_count`: the first tile of every slab uses all 8 entries.
All inputs are finite; a program needn't handle non-finite values.
Results may differ from a plain program's by a relative error of at most 0.0048.
Values may be sent and summed in bfloat16 or wider, within the bound.
A program may use at most 128 MiB of HBM per device.

v0:
```python
import jax
import jax.numpy as jnp
from jax import lax
from jax.sharding import PartitionSpec as P

HEADS = 12
HDIM = 128
TILE = 128
TPD = 4
NB = 8


masked_score = -1e30


def extended(x, sides, width):
    for axis, dim in sides:
        count, length = (lax.axis_size(axis), x.shape[dim])
        up = [(i, (i + 1) % count) for i in range(count - 1)]
        down = [(j, i) for i, j in up]
        last = lax.slice_in_dim(x, length - width, length, axis=dim)
        leading = lax.slice_in_dim(x, 0, width, axis=dim)
        before = lax.ppermute(last, axis, up)
        after = lax.ppermute(leading, axis, down)
        x = jnp.concatenate([before, x, after], axis=dim)
    return x


def on_device(
    queries, key_value, text_kv, residual, gate, bias, proj_weight, block_list, block_count
):
    query_rows = queries[0]
    row_count = query_rows.shape[0]
    slab_index = lax.axis_index("slab")
    nearby = extended(key_value[:, 0], (("slab", 1),), row_count)
    prompt_side = lax.all_gather(text_kv[:, 0], "slab", axis=1, tiled=True)
    text_count = prompt_side.shape[1]
    keys_all = jnp.concatenate([nearby[0], prompt_side[0]], 0)
    values_all = jnp.concatenate([nearby[1], prompt_side[1]], 0)
    first_tile = (slab_index - 1) * TPD
    candidate = first_tile + jnp.arange(3 * TPD, dtype=jnp.int32)
    usable = jnp.arange(NB, dtype=jnp.int32)[None, :] < block_count[:, None]
    member = jnp.any(
        (block_list[:, :, None] == candidate[None, None, :]) & usable[:, :, None], axis=1
    )
    tile_mask = jnp.repeat(jnp.repeat(member, TILE, axis=0), TILE, axis=1)
    allowed = jnp.concatenate([tile_mask, jnp.ones((row_count, text_count), dtype=bool)], 1)
    score_scale = HDIM ** (-0.5)

    def one_head(head_index):
        column_start = head_index * HDIM
        query_head = lax.dynamic_slice_in_dim(query_rows, column_start, HDIM, 1)
        key_head = lax.dynamic_slice_in_dim(keys_all, column_start, HDIM, 1)
        value_head = lax.dynamic_slice_in_dim(values_all, column_start, HDIM, 1)
        scores = lax.dot_general(
            query_head, key_head, (((1,), (1,)), ((), ())), preferred_element_type=jnp.float32
        )
        scores = jnp.where(allowed, scores * score_scale, masked_score)
        row_max = jnp.max(scores, axis=1, keepdims=True)
        exponent = jnp.where(allowed, jnp.exp(scores - row_max), 0.0)
        row_total = jnp.sum(exponent, axis=1, keepdims=True)
        weighted = jnp.dot(
            exponent.astype(jnp.bfloat16), value_head, preferred_element_type=jnp.float32
        )
        return (weighted / row_total).astype(jnp.bfloat16)

    per_head = lax.map(one_head, jnp.arange(HEADS, dtype=jnp.int32))
    attended = jnp.transpose(per_head, (1, 0, 2)).reshape(row_count, HEADS * HDIM)
    projected = jnp.dot(
        attended,
        lax.all_gather(proj_weight, "prompt", axis=0, tiled=True),
        preferred_element_type=jnp.float32,
    )
    result = residual[0].astype(jnp.float32) + gate[0][None, :] * (projected + bias[None, :])
    return result.astype(jnp.bfloat16)[None]


def solution(mesh):
    placed = (
        P("prompt", "slab", None),
        P(None, "prompt", "slab", None),
        P(None, "prompt", "slab", None),
        P("prompt", "slab", None),
        P("prompt", None),
        P(),
        P("prompt", None),
        P("slab", None),
        P("slab"),
    )
    return jax.shard_map(
        on_device, mesh=mesh, in_specs=placed, out_specs=P("prompt", "slab", None), check_vma=False
    )
```

profile of v0, /device:TPU:1, one launch (start us, length us, event | category | flops | bytes accessed | tf_op | source)
XLA Modules:
  0.0 203.1 jit_solution(6560510338463504875)
XLA Ops:
  6.5 0.7 all-gather.6.cloned.1.call-update
  7.3 4.5 %collective-permute-start = (bf16[2,512,1536]{2,1,0:T(8,128)(2,1)}, bf16[2,512,1536]{2,1,0:T(8,128)(2,1)}, u32[]{:S(2)}, u32[]{:S(2)}) collective-permute-start(bf16[2,512,1536]{2,1,0:T(8,128)(2,1)} %bitcast.35), channel_id=1, source_target_pairs={{0,1},{1,2},{2,3},{3,4},{4,5},{5,6},{6,7},{7,8},{8,9},{9,10},{10,1... | collective-permute-start | bytes 9437192 | tf_op jit(solution)/shard_map/ppermute | solution.py:23
  11.8 3.6 %collective-permute-start.1 = (bf16[2,512,1536]{2,1,0:T(8,128)(2,1)}, bf16[2,512,1536]{2,1,0:T(8,128)(2,1)}, u32[]{:S(2)}, u32[]{:S(2)}) collective-permute-start(bf16[2,512,1536]{2,1,0:T(8,128)(2,1)} %bitcast.36), channel_id=1, source_target_pairs={{1,0},{2,1},{3,2},{4,3},{5,4},{6,5},{7,6},{8,7},{9,8},{10,9},{11,1... | collective-permute-start | bytes 9437192 | tf_op jit(solution)/shard_map/ppermute | solution.py:24
  15.5 0.7 iota_compare_fusion
  16.2 0.8 and_reduce_fusion
  17.4 0.9 copy.17
  18.3 0.7 concatenate.14.clone
  19.0 54.1 %all-gather.6.cloned.1.call-done = bf16[2,1,256,1536]{3,2,1,0:T(8,128)(2,1)} async-done(((bf16[2,1,16,1536]{3,2,1,0:T(8,128)(2,1)}), bf16[2,1,256,1536]{3,2,1,0:T(8,128)(2,1)}) %all-gather.6.cloned.1.call-update) | async-done | bytes 1572880 | tf_op jit(solution)/shard_map/all_gather | solution.py:36
  73.2 1.6 slice_bitcast_fusion.2
  74.8 0.7 copy-done
  75.5 6.8 %pad_maximum_fusion = bf16[2,1536,1536]{2,1,0:T(8,128)(2,1)} fusion(bf16[2,512,1536]{2,1,0:T(8,128)(2,1)} %collective-permute-done.1, bf16[2,512,1536]{2,1,0:T(8,128)(2,1)S(1)} %bitcast.37, bf16[2,512,1536]{2,1,0:T(8,128)(2,1)} %collective-permute-done), kind=kLoop, calls=%fused_computation.17 | loop fusion | flops 28311552 | bytes 18874368 | tf_op jit(solution)/shard_map/concatenate | solution.py:25
  82.3 6.7 %slice_bitcast_fusion = (bf16[1536,1536]{1,0:T(8,128)(2,1)S(1)}, bf16[1536,1536]{1,0:T(8,128)(2,1)}) fusion(bf16[2,1536,1536]{2,1,0:T(8,128)(2,1)} %pad_maximum_fusion), kind=kLoop, calls=%fused_computation.22 | loop fusion | bytes 18874368 | tf_op jit(solution)/shard_map/squeeze | solution.py:39
  89.0 6.5 %pad_maximum_fusion.1 = (bf16[1792,1536]{1,0:T(8,128)(2,1)}, bf16[1792,1536]{1,0:T(8,128)(2,1)}) fusion(bf16[256,1536]{1,0:T(8,128)(2,1)S(1)} %get-tuple-element.76, bf16[1536,1536]{1,0:T(8,128)(2,1)} %get-tuple-element.74, bf16[256,1536]{1,0:T(8,128)(2,1)S(1)} %get-tuple-element.75, bf16[1536,1536]{1,0:T(8,128)(2,1)S(1)} %get-tuple-element.73), kind=kLoop, calls=%fused_computation.20 | loop fusion | flops 22020096 | bytes 22020096 | tf_op jit(solution)/shard_map/concatenate | solution.py:38
  95.5 75.7 %while.10 = (s32[]{:T(128)}, bf16[12,512,128]{1,2,0:T(8,128)(2,1)S(1)}, s32[12]{0:T(128)S(1)}, bf16[512,1536]{1,0:T(8,128)(2,1)}, bf16[1792,1536]{1,0:T(8,128)(2...) while((s32[]{:T(128)}, ...), condition=%wide.region_4.5_spmd, body=%wide.region_1.4_spmd.sunk | while | flops 478149632 | bytes 15477935 | solution.py:67
  95.5 0.6 dynamic_slice.30
  96.8 2.0 fusion.33
  98.8 1.0 fusion.34
  99.7 1.9 fusion.35
  101.8 0.6 dynamic_slice.30
  103.1 2.0 fusion.33
  105.1 1.0 fusion.34
  106.0 1.9 fusion.35
  108.1 0.6 dynamic_slice.30
  109.4 2.0 fusion.33
  111.4 1.0 fusion.34
  112.3 1.9 fusion.35
  114.4 0.6 dynamic_slice.30
  115.7 2.0 fusion.33
  117.7 1.0 fusion.34
  118.6 1.9 fusion.35
  120.7 0.6 dynamic_slice.30
  122.0 2.0 fusion.33
  124.0 1.0 fusion.34
  124.9 1.9 fusion.35
  127.0 0.6 dynamic_slice.30
  128.3 2.0 fusion.33
  130.3 1.0 fusion.34
  131.3 1.9 fusion.35
  133.3 0.6 dynamic_slice.30
  134.6 2.0 fusion.33
  136.6 1.0 fusion.34
  137.6 1.9 fusion.35
  139.7 0.6 dynamic_slice.30
  140.9 2.0 fusion.33
  142.9 1.0 fusion.34
  143.9 1.9 fusion.35
  146.0 0.6 dynamic_slice.30
  147.2 2.0 fusion.33
  149.2 1.0 fusion.34
  150.2 1.9 fusion.35
  152.3 0.6 dynamic_slice.30
  153.5 2.0 fusion.33
  155.5 1.0 fusion.34
  156.5 1.9 fusion.35
  158.6 0.6 dynamic_slice.30
  159.8 2.0 fusion.33
  161.8 1.0 fusion.34
  162.8 1.9 fusion.35
  164.9 0.6 dynamic_slice.30
  166.1 2.0 fusion.33
  168.1 1.0 fusion.34
  169.1 1.9 fusion.35
  171.2 13.7 %all-gather.4.cloned.1.call-done = bf16[1536,3072]{1,0:T(8,128)(2,1)} async-done(((bf16[96,3072]{1,0:T(8,128)(2,1)}), bf16[1536,3072]{1,0:T(8,128)(2,1)}) %all-gather.4.cloned.1.call-update) | async-done | bytes 9437200 | tf_op jit(solution)/shard_map/all_gather | solution.py:71
  184.9 11.3 %fusion.22 = bf16[1,512,3072]{2,1,0:T(8,128)(2,1)} fusion(bf16[512,1536]{0,1:T(8,128)(2,1)S(1)} %bitcast.42, bf16[1536,3072]{1,0:T(8,128)(2,1)} %all-gather.4.cloned.1.call-done, bf16[1,512,3072]{2,1,0:T(8,128)(2,1)} %param.14, f32[3072]{0:T(1024)S(1)} %copy-done.1, f32[3072]{0:T(1024)S(1)} %bitcast.43), kind=kOutput, calls=%fused_computation.24 | convolution fusion | flops 4839702528 | bytes 17326080 | tf_op jit(solution)/shard_map/dot_general | solution.py:69
  (42 shorter events, 2.1 us)
Async XLA Ops:
  6.5 66.6 %all-gather.6.cloned.1.call-start = ((), (), s32[]{:S(2)}) async-start(), calls=%async_computation.1 | async-start | bytes 1671168 | tf_op jit(solution)/shard_map/all_gather | solution.py:36
  7.3 177.7 %all-gather.4.cloned.1.call-start = ((), (), s32[]{:S(2)}) async-start(), calls=%async_computation | async-start | bytes 10027008 | tf_op jit(solution)/shard_map/all_gather | solution.py:71
  7.3 67.5 %collective-permute-start = (bf16[2,512,1536]{2,1,0:T(8,128)(2,1)}, bf16[2,512,1536]{2,1,0:T(8,128)(2,1)}, u32[]{:S(2)}, u32[]{:S(2)}) collective-permute-start(bf16[2,512,1536]{2,1,0:T(8,128)(2,1)} %bitcast.35), channel_id=1, source_target_pairs={{0,1},{1,2},{2,3},{3,4},{4,5},{5,6},{6,7},{7,8},{8,9},{9,10},{10,1... | collective-permute-start | bytes 9437192 | tf_op jit(solution)/shard_map/ppermute | solution.py:23
  11.8 63.0 %collective-permute-start.1 = (bf16[2,512,1536]{2,1,0:T(8,128)(2,1)}, bf16[2,512,1536]{2,1,0:T(8,128)(2,1)}, u32[]{:S(2)}, u32[]{:S(2)}) collective-permute-start(bf16[2,512,1536]{2,1,0:T(8,128)(2,1)} %bitcast.36), channel_id=1, source_target_pairs={{1,0},{2,1},{3,2},{4,3},{5,4},{6,5},{7,6},{8,7},{9,8},{10,9},{11,1... | collective-permute-start | bytes 9437192 | tf_op jit(solution)/shard_map/ppermute | solution.py:24
  73.2 2.4 %copy-start = (bf16[2,1,512,1536]{3,2,1,0:T(8,128)(2,1)S(1)}, bf16[2,1,512,1536]{3,2,1,0:T(8,128)(2,1)}, u32[]{:S(2)}) copy-start(bf16[2,1,512,1536]{3,2,1,0:T(8,128)(2,1)} %param.12) | copy-start | bytes 9437188
  95.5 89.4 %copy-start.1 = (f32[3072]{0:T(1024)S(1)}, f32[3072]{0:T(1024)}, u32[]{:S(2)}) copy-start(f32[3072]{0:T(1024)} %param.16) | copy-start | bytes 36868
  95.5 89.4 %copy-start.2 = (f32[1,3072]{1,0:T(1,128)S(1)}, f32[1,3072]{1,0:T(1,128)}, u32[]{:S(2)}) copy-start(f32[1,3072]{1,0:T(1,128)} %param.15) | copy-start | bytes 36868
Sparse Core Ops, SparseCore 0:
  10.1 62.9 all-gather.5
  74.9 109.9 all-gather.3
where the time goes:
time: 204 us; the launch traced here: 203 us
  waiting for transfers between devices  68.6 us (34%)
  matrix products  58.3 us (29%)
  other arithmetic  26.7 us (13%)
  local copies, waits for them, and re-layouts  19.8 us (10%)
  between operations  13.5 us (7%)
  starting transfers between devices  8.14 us (4%)
  loops' own time  8.06 us (4%)
    all_gather x1, waiting for transfers between devices, on_device(): prompt_side = lax.all_gather(text_kv[:, 0], 'slab', axis=1, tiled=True)  54.1 us
    dot_general x12, matrix products, one_head(): lax.dot_general(query_head, key_head, (((1,), (1,)), ((), ())), preferred...  23.8 us
    dot_general x12, matrix products, one_head(): jnp.dot(exponent.astype(jnp.bfloat16), value_head, preferred_element_type...  23.1 us
    all_gather x1, waiting for transfers between devices, on_device(): lax.all_gather(proj_weight, 'prompt', axis=0, tiled=True)  13.7 us
    reduce_sum x12, other arithmetic, one_head(): row_total = jnp.sum(exponent, axis=1, keepdims=True)  11.9 us
    dot_general x1, matrix products, on_device(): jnp.dot(attended, lax.all_gather(proj_weight, 'prompt', axis=0, tiled=Tru...  11.3 us
    squeeze x2, local copies, waits for them, and re-layouts, on_device(): values_all = jnp.concatenate([nearby[1], prompt_side[1]], 0)  8.34 us
    another operation x1, loops' own time, on_device(): per_head = lax.map(one_head, jnp.arange(HEADS, dtype=jnp.int32))  8.06 us
  transfers between devices with their start and end apart: 4, of which 2 were waited for; matrix products, arithmetic and copies ran while one was open for 46% of the time, Pallas kernels for 0%

commit v1 on v0

v1 whole, which is shorter than its diff:
```python
import functools

import jax
import jax.numpy as jnp
from jax import lax
from jax.experimental import pallas as pl
from jax.experimental.pallas import tpu as pltpu
from jax.sharding import PartitionSpec as P

MESH = pl.DeviceIdType.MESH
HEADS = 12
HDIM = 128
TILE = 128
TPD = 4
NB = 8
ROWS = 512
HD = 1536
D = 3072
TXT = 256
SHARD = 96
HALF = 48
BLOCK = 256
OUT_COLS = 512
SIDE = 768
PART = 1536
masked_score = -1e30
EXP2_SCALE = HDIM**-0.5 * 1.4426950408889634
CONTRACT_LAST = (((1,), (1,)), ((), ()))


def attend_head(head, q, kvb, txt, mask, att):
    col = pl.ds(pl.multiple_of(head * HDIM, HDIM), HDIM)
    for start in range(0, ROWS, BLOCK):
        rows = q[pl.ds(start, BLOCK), col]
        parts = []
        for source in range(3):
            scores = lax.dot_general(
                rows, kvb[source, 0, :, col], CONTRACT_LAST, preferred_element_type=jnp.float32
            )
            tiles = []
            for t in range(BLOCK // TILE):
                at = start // TILE + t
                tiles.append(
                    scores[t * TILE : (t + 1) * TILE]
                    + mask[at : at + 1, source * ROWS : (source + 1) * ROWS]
                )
            parts.append(jnp.concatenate(tiles, 0))
        parts.append(
            lax.dot_general(rows, txt[0, :, col], CONTRACT_LAST, preferred_element_type=jnp.float32)
        )
        largest = functools.reduce(
            jnp.maximum, [jnp.max(part, axis=1, keepdims=True) for part in parts]
        )
        shift = largest * EXP2_SCALE
        total, weighted = None, None
        for i, part in enumerate(parts):
            weights = jnp.exp2(part * EXP2_SCALE - shift)
            part_total = jnp.sum(weights, axis=1, keepdims=True)
            values = kvb[i, 1, :, col] if i < 3 else txt[1, :, col]
            part_weighted = jnp.dot(
                weights.astype(jnp.bfloat16), values, preferred_element_type=jnp.float32
            )
            total = part_total if i == 0 else total + part_total
            weighted = part_weighted if i == 0 else weighted + part_weighted
        att[pl.ds(start, BLOCK), col] = (weighted / total).astype(jnp.bfloat16)


def kernel(
    q_hbm,
    kv_hbm,
    t_hbm,
    res_hbm,
    gate,
    bias,
    w_hbm,
    block_list,
    block_count,
    out_hbm,
    q,
    kvb,
    txt,
    wfull,
    mask,
    att,
    acc,
    res,
    local_sem,
    out_sem,
    kvx_send,
    kvx_recv,
    kvc_send,
    kvc_recv,
    text_send,
    text_recv,
    wz_send,
    wz_recv,
    wy_send,
    wy_recv,
    wp_send,
    wp_recv,
):
    p, s = lax.axis_index("prompt"), lax.axis_index("slab")
    y_lo, z = p // 8, p % 8
    y_hi, x, c = s // 8, (s % 8) // 2, s % 2
    y = y_hi * 2 + y_lo

    def device(x, y, z, c):
        return {"prompt": (y % 2) * 8 + z, "slab": (y // 2) * 8 + x * 2 + c}

    partner = device(x, y, z, 1 - c)
    far = s - 1 + 2 * c
    has_far = (far >= 0) & (far < 16)
    far_device = {"prompt": p, "slab": jnp.clip(far, 0, 15)}
    along = 1 - 2 * c
    z_of = lambda k: lax.rem(z + along * k + 8, 8)
    z_next, z_prev = device(x, y, z_of(1), c), device(x, y, z_of(-1), c)
    y_next, y_prev = device(x, lax.rem(y + 1, 4), z, c), device(x, lax.rem(y + 3, 4), z, c)
    both_y = ((x == 0) & (y_hi == 1)) | ((x == 3) & (y_hi == 0))
    inner = (x == 1) | (x == 2)
    up_y, down_y = both_y | (inner & (y_lo == 0)), both_y | (inner & (y_lo == 1))
    head_of = lambda i: lax.rem(i + y_lo * 6, HEADS)
    chips = [(dx, dy) for dy in (0, 2) for dx in range(4) if dx or dy]
    clip_chips = [
        device(lax.rem(x + dx, 4), lax.rem(y + dy, 4), z, c) for dx, dy in chips
    ]
    middle = (s == 7) | (s == 8)

    barrier = pltpu.get_barrier_semaphore()
    fixed = [partner, z_next, z_prev, y_next, y_prev] + clip_chips
    for target in fixed:
        pl.semaphore_signal(barrier, inc=1, device_id=target, device_id_type=MESH)

    @pl.when(has_far)
    def _():
        pl.semaphore_signal(barrier, inc=1, device_id=far_device, device_id_type=MESH)

    text_own = pl.ds(pl.multiple_of(((c * 2 + y_hi) * 4 + x) * 16, 16), 16)
    copy_q = pltpu.make_async_copy(q_hbm, q, local_sem.at[0])
    copy_kv = pltpu.make_async_copy(kv_hbm, kvb.at[0], local_sem.at[1])
    copy_text = pltpu.make_async_copy(t_hbm, txt.at[:, text_own, :], local_sem.at[2])
    copy_w = pltpu.make_async_copy(
        w_hbm, wfull.at[pl.ds(pl.multiple_of(p * SHARD, SHARD), SHARD)], local_sem.at[3]
    )
    copy_res = pltpu.make_async_copy(res_hbm, res, local_sem.at[4])
    copy_edge = pltpu.make_async_copy(kv_hbm, kvb.at[2], local_sem.at[5])
    for copy in (copy_text, copy_kv, copy_q, copy_w, copy_res):
        copy.start()

    @pl.when(jnp.logical_not(has_far))
    def _():
        copy_edge.start()

    lane = lax.broadcasted_iota(jnp.int32, (1, 3 * ROWS), 1)
    slab_of = jnp.where(lane < ROWS, s, jnp.where(lane < 2 * ROWS, s + 1 - 2 * c, far))
    tile_of = slab_of * TPD + lax.rem(lane, ROWS) // TILE
    for t in range(TPD):
        member = None
        for n in range(NB):
            listed = jnp.where(n < block_count[t], block_list[t, n], -1000)
            match = tile_of == listed
            member = match if n == 0 else member | match
        mask[t : t + 1, :] = jnp.where(member, 0.0, masked_score)

    pl.semaphore_wait(barrier, len(fixed) + has_far.astype(jnp.int32))

    def remote(src, dst, send_sem, recv_sem, to):
        return pltpu.make_async_remote_copy(
            src_ref=src,
            dst_ref=dst,
            send_sem=send_sem,
            recv_sem=recv_sem,
            device_id=to,
            device_id_type=MESH,
        )

    text_half = pl.ds(pl.multiple_of(c * 128, 128), 128)

    def text_out(i):
        return remote(
            t_hbm, txt.at[:, text_own, :], text_send.at[i], text_recv.at[i], clip_chips[i]
        )

    def text_partner():
        block = txt.at[:, text_half, :]
        return remote(block, block, text_send.at[7], text_recv.at[7], partner)

    def w_block(side, z_at, core, part):
        start = (side * 8 + z_at) * SHARD + core * HALF
        return wfull.at[pl.ds(pl.multiple_of(start, 16), HALF), pl.ds(part * PART, PART)]

    def w_own(part):
        return w_hbm.at[pl.ds(pl.multiple_of(c * HALF, 16), HALF), pl.ds(part * PART, PART)]

    sides, parts = (y_lo, y_lo, 1 - y_lo), (0, 1, 1)

    def w_z(stream, slot):
        offset = -slot if slot < 4 else slot - 4
        dst = w_block(sides[stream], z_of(offset), c, parts[stream])
        src = w_own(parts[stream]) if stream < 2 and offset == 0 else dst
        at = stream * 7 + slot
        return remote(src, dst, wz_send.at[at], wz_recv.at[at], z_next if slot < 4 else z_prev)

    def w_z_partner(stream, offset):
        block = w_block(sides[stream], z_of(offset), c, parts[stream])
        at = stream * 7 + (-offset - 1 if offset < 0 else 3 + offset)
        return remote(block, block, wp_send.at[at], wp_recv.at[at], partner)

    across_offsets = [0, 0, -1, 1, -2, 2, -3, 3, -4]

    def w_y(i, up):
        part = 1 if i == 0 else 0
        dst = w_block(y_lo, z_of(across_offsets[i]), c, part)
        src = w_own(part) if i < 2 else dst
        at = i if up else 9 + i
        return remote(src, dst, wy_send.at[at], wy_recv.at[i], y_next if up else y_prev)

    def w_y_partner(i):
        block = w_block(1 - y_lo, z_of(across_offsets[i]), c, 1 if i == 0 else 0)
        return remote(block, block, wp_send.at[21 + i], wp_recv.at[21 + i], partner)

    def send_y(i):
        pl.when(up_y)(lambda: w_y(i, True).start())
        pl.when(down_y)(lambda: w_y(i, False).start())

    def kv_cols(h):
        if isinstance(h, int):
            return pl.ds(h * HDIM, HDIM)
        return pl.ds(pl.multiple_of(h * HDIM, HDIM), HDIM)

    def kv_far(h):
        return remote(
            kv_hbm.at[:, :, kv_cols(h)],
            kvb.at[2, :, :, kv_cols(h)],
            kvx_send.at[h],
            kvx_recv.at[h],
            far_device,
        )

    def kv_near(h):
        return remote(
            kv_hbm.at[:, :, kv_cols(h)],
            kvb.at[1, :, :, kv_cols(h)],
            kvc_send.at[h],
            kvc_recv.at[h],
            partner,
        )

    def send_far():
        @pl.when(has_far)
        def _():
            for i in range(HEADS):
                kv_far(head_of(i)).start()

    for i in range(7):
        text_out(i).start()
    w_z(0, 0).start()
    w_z(0, 4).start()
    send_y(0)
    pl.when(jnp.logical_not(middle))(lambda: send_far())
    w_z(1, 0).start()
    w_z(1, 4).start()
    send_y(1)
    kv_near(head_of(0)).start()
    kv_near(head_of(1)).start()

    copy_text.wait()
    copy_kv.wait()
    copy_q.wait()
    copy_w.wait()
    copy_res.wait()

    @pl.when(jnp.logical_not(has_far))
    def _():
        copy_edge.wait()

    def text_first():
        for i in range(7):
            text_out(i).wait_recv()
        text_partner().start()
        pl.when(middle)(lambda: send_far())

    def ring(stream, d):
        w_z(stream, d - 1).wait_recv()
        if d < 4:
            w_z(stream, d).start()
        if stream == 0:
            send_y(2 * d)
        w_z_partner(stream, -d).start()
        if d < 4:
            w_z(stream, 3 + d).wait_recv()
            if d < 3:
                w_z(stream, 4 + d).start()
            if stream == 0:
                send_y(2 * d + 1)
            w_z_partner(stream, d).start()

    def across(*slots):
        for i in slots:
            w_y(i, True).wait_recv()
            if i == 0:
                w_z(2, 0).start()
                w_z(2, 4).start()
            w_y_partner(i).start()

    events = {
        0: [
            lambda: across(0),
            lambda: ring(0, 1),
            lambda: text_first(),
            lambda: ring(1, 1),
            lambda: ring(2, 1),
            lambda: text_partner().wait_recv(),
        ],
        1: [lambda: ring(0, 2), lambda: across(1, 2, 3)],
        2: [lambda: ring(1, 2)],
        4: [lambda: ring(2, 2)],
        5: [lambda: ring(0, 3), lambda: across(4, 5)],
        6: [lambda: ring(1, 3)],
        7: [lambda: ring(2, 3)],
        8: [lambda: ring(0, 4), lambda: across(6, 7)],
        9: [lambda: ring(1, 4)],
        10: [lambda: ring(2, 4), lambda: across(8)],
    }
    own_side = pl.ds(pl.multiple_of(y_lo * SIDE, SIDE), SIDE)
    other_side = pl.ds(pl.multiple_of((1 - y_lo) * SIDE, SIDE), SIDE)

    def project_own():
        for stream in range(2):
            for d in (-4, -3, -2, -1, 1, 2, 3):
                w_z_partner(stream, d).wait_recv()

        def column(j, _):
            cols = pl.ds(pl.multiple_of(j * OUT_COLS, OUT_COLS), OUT_COLS)
            acc[:, cols] = jnp.dot(
                att[:, own_side], wfull[own_side, cols], preferred_element_type=jnp.float32
            )
            return 0

        lax.fori_loop(0, D // OUT_COLS, column, 0)

    def step(h, _):
        for at, actions in events.items():

            @pl.when(h == at)
            def _():
                for action in actions:
                    action()

        @pl.when(h < HEADS - 2)
        def _():
            kv_near(head_of(h + 2)).start()

        head = head_of(h)
        kv_near(head).wait_recv()

        @pl.when(has_far)
        def _():
            kv_far(head).wait_recv()

        attend_head(head, q, kvb, txt, mask, att)

        @pl.when(h == 10)
        def _():
            project_own()

        return 0

    lax.fori_loop(0, HEADS, step, 0)
    for d in (-4, -3, -2, -1, 1, 2, 3):
        w_z_partner(2, d).wait_recv()
    for i in range(9):
        w_y_partner(i).wait_recv()

    def copy_out(j):
        cols = pl.ds(pl.multiple_of(j * OUT_COLS, OUT_COLS), OUT_COLS)
        return pltpu.make_async_copy(res.at[:, cols], out_hbm.at[:, cols], out_sem.at[j])

    def finish(j, _):
        cols = pl.ds(pl.multiple_of(j * OUT_COLS, OUT_COLS), OUT_COLS)
        projected = acc[:, cols] + jnp.dot(
            att[:, other_side], wfull[other_side, cols], preferred_element_type=jnp.float32
        )
        result = res[:, cols].astype(jnp.float32) + gate[:, cols] * (projected + bias[:, cols])
        res[:, cols] = result.astype(jnp.bfloat16)
        copy_out(j).start()
        return 0

    lax.fori_loop(0, D // OUT_COLS, finish, 0)

    for i in range(7):
        text_out(i).wait_send()
    text_partner().wait_send()
    for stream in range(3):
        for slot in range(7):
            w_z(stream, slot).wait_send()
        for d in (-4, -3, -2, -1, 1, 2, 3):
            w_z_partner(stream, d).wait_send()
    for i in range(9):
        w_y_partner(i).wait_send()

    @pl.when(up_y)
    def _():
        for i in range(9):
            w_y(i, True).wait_send()

    @pl.when(down_y)
    def _():
        for i in range(9):
            w_y(i, False).wait_send()


    def sent(h, _):
        kv_near(h).wait_send()

        @pl.when(has_far)
        def _():
            kv_far(h).wait_send()

        return 0

    lax.fori_loop(0, HEADS, sent, 0)
    lax.fori_loop(0, D // OUT_COLS, lambda j, _: (copy_out(j).wait(), 0)[1], 0)


def on_device(
    queries, key_value, text_kv, residual, gate, bias, proj_weight, block_list, block_count
):
    hbm = pl.BlockSpec(memory_space=pl.ANY)
    vmem = pl.BlockSpec(memory_space=pltpu.VMEM)
    smem = pl.BlockSpec(memory_space=pltpu.SMEM)
    dma = pltpu.SemaphoreType.DMA
    result = pl.pallas_call(
        kernel,
        out_shape=jax.ShapeDtypeStruct((ROWS, D), jnp.bfloat16),
        in_specs=[hbm, hbm, hbm, hbm, vmem, vmem, hbm, smem, smem],
        out_specs=hbm,
        scratch_shapes=[
            pltpu.VMEM((ROWS, HD), jnp.bfloat16),
            pltpu.VMEM((3, 2, ROWS, HD), jnp.bfloat16),
            pltpu.VMEM((2, TXT, HD), jnp.bfloat16),
            pltpu.VMEM((HD, D), jnp.bfloat16),
            pltpu.VMEM((TPD, 3 * ROWS), jnp.float32),
            pltpu.VMEM((ROWS, HD), jnp.bfloat16),
            pltpu.VMEM((ROWS, D), jnp.float32),
            pltpu.VMEM((ROWS, D), jnp.bfloat16),
            dma((6,)),
            dma((D // OUT_COLS,)),
            dma((HEADS,)),
            dma((HEADS,)),
            dma((HEADS,)),
            dma((HEADS,)),
            dma((8,)),
            dma((8,)),
            dma((21,)),
            dma((21,)),
            dma((18,)),
            dma((9,)),
            dma((30,)),
            dma((30,)),
        ],
        compiler_params=pltpu.CompilerParams(
            collective_id=0, has_side_effects=True, vmem_limit_bytes=60 * 2**20
        ),
    )(
        queries[0],
        key_value[:, 0],
        text_kv[:, 0],
        residual[0],
        gate,
        bias[None],
        proj_weight,
        block_list,
        block_count,
    )
    return result[None]


def solution(mesh):
    placed = (
        P("prompt", "slab", None),
        P(None, "prompt", "slab", None),
        P(None, "prompt", "slab", None),
        P("prompt", "slab", None),
        P("prompt", None),
        P(),
        P("prompt", None),
        P("slab", None),
        P("slab"),
    )
    return jax.shard_map(
        on_device, mesh=mesh, in_specs=placed, out_specs=P("prompt", "slab", None), check_vma=False
    )
```

time: 204 us -> 75 us (0.37)
  the two profiles are of different devices: /device:TPU:1 before, /device:TPU:7 now
where the time goes in v1:
time: 75 us; the launch traced here: 74.9 us
  Pallas kernels  71.1 us (95%)
  local copies, waits for them, and re-layouts  3.76 us (5%)
    pallas_call x1, Pallas kernels, on_device(): pl.pallas_call(kernel, out_shape=jax.ShapeDtypeStruct((ROWS, D), jnp.bflo...  71.1 us
    unnamed x1, local copies, waits for them, and re-layouts  3.76 us

profile of v1, /device:TPU:7, one launch (start us, length us, event | category | flops | bytes accessed | tf_op | source)
XLA Modules:
  0.0 74.9 jit_solution(10400384230257105337)
XLA Ops:
  0.0 71.1 %shard_map.91 = bf16[512,3072]{1,0:T(8,128)(2,1)} custom-call(bf16[512,1536]{1,0:T(8,128)(2,1)} %bitcast.9, bf16[2,512,1536]{2,1,0:T(8,128)(2,1)} %bitcast.7, bf16[2,16,1536]{2,1,0:T(8,128)(2,1)} %bitcast.10, bf16[512,3072]{1,0:T(8,128)(2,1)} %bitcast.8, f32[1,3072]{1,0:T(1,128)} %gate.1, f32[1,3072]{1,0:T(1,128)} %bitcast.11, bf16[96,3072]{1,0:T(8,128)(2,1)} %w_hbm.1, ...), custom_call_target="tpu_custom_call" | custom-call | tf_op jit(solution)/shard_map/pallas_call | solution.py:432
  71.1 3.8 %copy.11 = bf16[1,512,3072]{2,1,0:T(8,128)(2,1)} copy(bf16[1,512,3072]{2,1,0:T(8,128)(2,1)} %bitcast.6) | data formatting | bytes 6291456

commit v2 on v1

--- a/solution.py
+++ b/solution.py
@@ -21,6 +21,7 @@
 HALF = 48
 BLOCK = 256
 OUT_COLS = 512
+BLOCKS = 3
 SIDE = 768
 PART = 1536
 masked_score = -1e30
@@ -119,14 +120,11 @@
     inner = (x == 1) | (x == 2)
     up_y, down_y = both_y | (inner & (y_lo == 0)), both_y | (inner & (y_lo == 1))
     head_of = lambda i: lax.rem(i + y_lo * 6, HEADS)
-    chips = [(dx, dy) for dy in (0, 2) for dx in range(4) if dx or dy]
-    clip_chips = [
-        device(lax.rem(x + dx, 4), lax.rem(y + dy, 4), z, c) for dx, dy in chips
-    ]
-    middle = (s == 7) | (s == 8)
+    y_far = device(x, lax.rem(y + 2, 4), z, c)
+    x_others = [device(lax.rem(x + dx, 4), y, z, c) for dx in (1, 2, 3)]
 
     barrier = pltpu.get_barrier_semaphore()
-    fixed = [partner, z_next, z_prev, y_next, y_prev] + clip_chips
+    fixed = [partner, z_next, z_prev, y_next, y_prev, y_far] + x_others
     for target in fixed:
         pl.semaphore_signal(barrier, inc=1, device_id=target, device_id_type=MESH)
 
@@ -135,6 +133,7 @@
         pl.semaphore_signal(barrier, inc=1, device_id=far_device, device_id_type=MESH)
 
     text_own = pl.ds(pl.multiple_of(((c * 2 + y_hi) * 4 + x) * 16, 16), 16)
+    text_over = pl.ds(pl.multiple_of(((c * 2 + 1 - y_hi) * 4 + x) * 16, 16), 16)
     copy_q = pltpu.make_async_copy(q_hbm, q, local_sem.at[0])
     copy_kv = pltpu.make_async_copy(kv_hbm, kvb.at[0], local_sem.at[1])
     copy_text = pltpu.make_async_copy(t_hbm, txt.at[:, text_own, :], local_sem.at[2])
@@ -175,10 +174,13 @@
 
     text_half = pl.ds(pl.multiple_of(c * 128, 128), 128)
 
-    def text_out(i):
-        return remote(
-            t_hbm, txt.at[:, text_own, :], text_send.at[i], text_recv.at[i], clip_chips[i]
-        )
+    def text_y():
+        return remote(t_hbm, txt.at[:, text_own, :], text_send.at[0], text_recv.at[0], y_far)
+
+    def text_x(i, over):
+        rows, at = (text_over, 4 + i) if over else (text_own, 1 + i)
+        src = txt.at[:, rows, :] if over else t_hbm
+        return remote(src, txt.at[:, rows, :], text_send.at[at], text_recv.at[at], x_others[i])
 
     def text_partner():
         block = txt.at[:, text_half, :]
@@ -251,12 +253,12 @@
             for i in range(HEADS):
                 kv_far(head_of(i)).start()
 
-    for i in range(7):
-        text_out(i).start()
+    text_y().start()
     w_z(0, 0).start()
     w_z(0, 4).start()
     send_y(0)
-    pl.when(jnp.logical_not(middle))(lambda: send_far())
+    for i in range(3):
+        text_x(i, False).start()
     w_z(1, 0).start()
     w_z(1, 4).start()
     send_y(1)
@@ -274,10 +276,16 @@
         copy_edge.wait()
 
     def text_first():
-        for i in range(7):
-            text_out(i).wait_recv()
+        text_y().wait_recv()
+        for i in range(3):
+            text_x(i, True).start()
+        send_far()
+
+    def text_second():
+        for i in range(3):
+            text_x(i, False).wait_recv()
+            text_x(i, True).wait_recv()
         text_partner().start()
-        pl.when(middle)(lambda: send_far())
 
     def ring(stream, d):
         w_z(stream, d - 1).wait_recv()
@@ -304,30 +312,31 @@
 
     events = {
         0: [
+            lambda: text_first(),
             lambda: across(0),
             lambda: ring(0, 1),
-            lambda: text_first(),
             lambda: ring(1, 1),
+            lambda: text_second(),
             lambda: ring(2, 1),
             lambda: text_partner().wait_recv(),
         ],
         1: [lambda: ring(0, 2), lambda: across(1, 2, 3)],
         2: [lambda: ring(1, 2)],
-        4: [lambda: ring(2, 2)],
-        5: [lambda: ring(0, 3), lambda: across(4, 5)],
-        6: [lambda: ring(1, 3)],
-        7: [lambda: ring(2, 3)],
-        8: [lambda: ring(0, 4), lambda: across(6, 7)],
-        9: [lambda: ring(1, 4)],
-        10: [lambda: ring(2, 4), lambda: across(8)],
+        3: [lambda: ring(2, 2)],
+        4: [lambda: ring(0, 3), lambda: across(4, 5)],
+        5: [lambda: ring(1, 3)],
+        6: [lambda: ring(2, 3)],
+        7: [lambda: ring(0, 4), lambda: across(6, 7)],
+        8: [lambda: ring(1, 4)],
+        9: [lambda: project_own(0), lambda: ring(2, 4)],
+        10: [lambda: project_own(1), lambda: across(8)],
     }
     own_side = pl.ds(pl.multiple_of(y_lo * SIDE, SIDE), SIDE)
     other_side = pl.ds(pl.multiple_of((1 - y_lo) * SIDE, SIDE), SIDE)
 
-    def project_own():
-        for stream in range(2):
-            for d in (-4, -3, -2, -1, 1, 2, 3):
-                w_z_partner(stream, d).wait_recv()
+    def project_own(part):
+        for d in (-4, -3, -2, -1, 1, 2, 3):
+            w_z_partner(part, d).wait_recv()
 
         def column(j, _):
             cols = pl.ds(pl.multiple_of(j * OUT_COLS, OUT_COLS), OUT_COLS)
@@ -336,7 +345,7 @@
             )
             return 0
 
-        lax.fori_loop(0, D // OUT_COLS, column, 0)
+        lax.fori_loop(part * BLOCKS, part * BLOCKS + BLOCKS, column, 0)
 
     def step(h, _):
         for at, actions in events.items():
@@ -359,17 +368,9 @@
 
         attend_head(head, q, kvb, txt, mask, att)
 
-        @pl.when(h == 10)
-        def _():
-            project_own()
-
         return 0
 
     lax.fori_loop(0, HEADS, step, 0)
-    for d in (-4, -3, -2, -1, 1, 2, 3):
-        w_z_partner(2, d).wait_recv()
-    for i in range(9):
-        w_y_partner(i).wait_recv()
 
     def copy_out(j):
         cols = pl.ds(pl.multiple_of(j * OUT_COLS, OUT_COLS), OUT_COLS)
@@ -385,10 +386,18 @@
         copy_out(j).start()
         return 0
 
-    lax.fori_loop(0, D // OUT_COLS, finish, 0)
-
-    for i in range(7):
-        text_out(i).wait_send()
+    w_y_partner(0).wait_recv()
+    for d in (-4, -3, -2, -1, 1, 2, 3):
+        w_z_partner(2, d).wait_recv()
+    lax.fori_loop(BLOCKS, 2 * BLOCKS, finish, 0)
+    for i in range(1, 9):
+        w_y_partner(i).wait_recv()
+    lax.fori_loop(0, BLOCKS, finish, 0)
+
+    text_y().wait_send()
+    for i in range(3):
+        text_x(i, False).wait_send()
+        text_x(i, True).wait_send()
     text_partner().wait_send()
     for stream in range(3):
         for slot in range(7):

time: 75 us -> 67.1 us (0.89)
  the two profiles are of different devices: /device:TPU:7 before, /device:TPU:1 now
where the time goes in v2:
time: 67.1 us; the launch traced here: 67 us
  Pallas kernels  63.2 us (94%)
  local copies, waits for them, and re-layouts  3.76 us (6%)
    pallas_call x1, Pallas kernels, on_device(): pl.pallas_call(kernel, out_shape=jax.ShapeDtypeStruct((ROWS, D), jnp.bflo...  63.2 us
    unnamed x1, local copies, waits for them, and re-layouts  3.76 us

profile of v2, /device:TPU:1, one launch (start us, length us, event | category | flops | bytes accessed | tf_op | source)
XLA Modules:
  0.0 67.0 jit_solution(13809244032807911883)
XLA Ops:
  0.0 63.2 %shard_map.91 = bf16[512,3072]{1,0:T(8,128)(2,1)} custom-call(bf16[512,1536]{1,0:T(8,128)(2,1)} %bitcast.9, bf16[2,512,1536]{2,1,0:T(8,128)(2,1)} %bitcast.7, bf16[2,16,1536]{2,1,0:T(8,128)(2,1)} %bitcast.10, bf16[512,3072]{1,0:T(8,128)(2,1)} %bitcast.8, f32[1,3072]{1,0:T(1,128)} %gate.1, f32[1,3072]{1,0:T(1,128)} %bitcast.11, bf16[96,3072]{1,0:T(8,128)(2,1)} %w_hbm.1, ...), custom_call_target="tpu_custom_call" | custom-call | tf_op jit(solution)/shard_map/pallas_call | solution.py:441
  63.2 3.8 %copy.11 = bf16[1,512,3072]{2,1,0:T(8,128)(2,1)} copy(bf16[1,512,3072]{2,1,0:T(8,128)(2,1)} %bitcast.6) | data formatting | bytes 6291456

commit v3 on v2

--- a/solution.py
+++ b/solution.py
@@ -29,38 +29,45 @@
 CONTRACT_LAST = (((1,), (1,)), ((), ()))
 
 
+def scores_of(rows, keys, start, mask, source):
+    scores = lax.dot_general(rows, keys, CONTRACT_LAST, preferred_element_type=jnp.float32)
+    tiles = []
+    for t in range(BLOCK // TILE):
+        at = start // TILE + t
+        tiles.append(
+            scores[t * TILE : (t + 1) * TILE]
+            + mask[at : at + 1, source * ROWS : (source + 1) * ROWS]
+        )
+    return jnp.concatenate(tiles, 0)
+
+
+def largest_of(parts):
+    return functools.reduce(jnp.maximum, [jnp.max(part, axis=1, keepdims=True) for part in parts])
+
+
+def weigh(part, shift, values):
+    weights = jnp.exp2(part * EXP2_SCALE - shift)
+    weighted = jnp.dot(weights.astype(jnp.bfloat16), values, preferred_element_type=jnp.float32)
+    return jnp.sum(weights, axis=1, keepdims=True), weighted
+
+
+def columns_of(head):
+    return pl.ds(pl.multiple_of(head * HDIM, HDIM), HDIM)
+
+
 def attend_head(head, q, kvb, txt, mask, att):
-    col = pl.ds(pl.multiple_of(head * HDIM, HDIM), HDIM)
+    col = columns_of(head)
     for start in range(0, ROWS, BLOCK):
         rows = q[pl.ds(start, BLOCK), col]
-        parts = []
-        for source in range(3):
-            scores = lax.dot_general(
-                rows, kvb[source, 0, :, col], CONTRACT_LAST, preferred_element_type=jnp.float32
-            )
-            tiles = []
-            for t in range(BLOCK // TILE):
-                at = start // TILE + t
-                tiles.append(
-                    scores[t * TILE : (t + 1) * TILE]
-                    + mask[at : at + 1, source * ROWS : (source + 1) * ROWS]
-                )
-            parts.append(jnp.concatenate(tiles, 0))
+        parts = [scores_of(rows, kvb[i, 0, :, col], start, mask, i) for i in range(3)]
         parts.append(
             lax.dot_general(rows, txt[0, :, col], CONTRACT_LAST, preferred_element_type=jnp.float32)
         )
-        largest = functools.reduce(
-            jnp.maximum, [jnp.max(part, axis=1, keepdims=True) for part in parts]
-        )
-        shift = largest * EXP2_SCALE
+        shift = largest_of(parts) * EXP2_SCALE
         total, weighted = None, None
         for i, part in enumerate(parts):
-            weights = jnp.exp2(part * EXP2_SCALE - shift)
-            part_total = jnp.sum(weights, axis=1, keepdims=True)
             values = kvb[i, 1, :, col] if i < 3 else txt[1, :, col]
-            part_weighted = jnp.dot(
-                weights.astype(jnp.bfloat16), values, preferred_element_type=jnp.float32
-            )
+            part_total, part_weighted = weigh(part, shift, values)
             total = part_total if i == 0 else total + part_total
             weighted = part_weighted if i == 0 else weighted + part_weighted
         att[pl.ds(start, BLOCK), col] = (weighted / total).astype(jnp.bfloat16)
@@ -76,7 +83,7 @@
     w_hbm,
     block_list,
     block_count,
-    out_hbm,
+    out,
     q,
     kvb,
     txt,
@@ -86,7 +93,6 @@
     acc,
     res,
     local_sem,
-    out_sem,
     kvx_send,
     kvx_recv,
     kvc_send,
@@ -247,10 +253,10 @@
             partner,
         )
 
-    def send_far():
+    def send_far(first, last):
         @pl.when(has_far)
         def _():
-            for i in range(HEADS):
+            for i in range(first, last):
                 kv_far(head_of(i)).start()
 
     text_y().start()
@@ -259,6 +265,7 @@
     send_y(0)
     for i in range(3):
         text_x(i, False).start()
+    send_far(0, 1)
     w_z(1, 0).start()
     w_z(1, 4).start()
     send_y(1)
@@ -279,7 +286,7 @@
         text_y().wait_recv()
         for i in range(3):
             text_x(i, True).start()
-        send_far()
+        send_far(1, HEADS)
 
     def text_second():
         for i in range(3):
@@ -328,8 +335,9 @@
         6: [lambda: ring(2, 3)],
         7: [lambda: ring(0, 4), lambda: across(6, 7)],
         8: [lambda: ring(1, 4)],
-        9: [lambda: project_own(0), lambda: ring(2, 4)],
-        10: [lambda: project_own(1), lambda: across(8)],
+        9: [lambda: ring(2, 4), lambda: project_own(0)],
+        10: [lambda: across(8)],
+        11: [lambda: project_own(1)],
     }
     own_side = pl.ds(pl.multiple_of(y_lo * SIDE, SIDE), SIDE)
     other_side = pl.ds(pl.multiple_of((1 - y_lo) * SIDE, SIDE), SIDE)
@@ -340,8 +348,11 @@
 
         def column(j, _):
             cols = pl.ds(pl.multiple_of(j * OUT_COLS, OUT_COLS), OUT_COLS)
-            acc[:, cols] = jnp.dot(
+            projected = jnp.dot(
                 att[:, own_side], wfull[own_side, cols], preferred_element_type=jnp.float32
+            )
+            acc[:, cols] = res[:, cols].astype(jnp.float32) + gate[:, cols] * (
+                projected + bias[:, cols]
             )
             return 0
 
@@ -367,23 +378,17 @@
             kv_far(head).wait_recv()
 
         attend_head(head, q, kvb, txt, mask, att)
-
         return 0
 
     lax.fori_loop(0, HEADS, step, 0)
-
-    def copy_out(j):
-        cols = pl.ds(pl.multiple_of(j * OUT_COLS, OUT_COLS), OUT_COLS)
-        return pltpu.make_async_copy(res.at[:, cols], out_hbm.at[:, cols], out_sem.at[j])
 
     def finish(j, _):
         cols = pl.ds(pl.multiple_of(j * OUT_COLS, OUT_COLS), OUT_COLS)
-        projected = acc[:, cols] + jnp.dot(
+        projected = jnp.dot(
             att[:, other_side], wfull[other_side, cols], preferred_element_type=jnp.float32
         )
-        result = res[:, cols].astype(jnp.float32) + gate[:, cols] * (projected + bias[:, cols])
-        res[:, cols] = result.astype(jnp.bfloat16)
-        copy_out(j).start()
+        result = acc[:, cols] + gate[:, cols] * projected
+        out[:, cols] = result.astype(jnp.bfloat16)
         return 0
 
     w_y_partner(0).wait_recv()
@@ -428,7 +433,6 @@
         return 0
 
     lax.fori_loop(0, HEADS, sent, 0)
-    lax.fori_loop(0, D // OUT_COLS, lambda j, _: (copy_out(j).wait(), 0)[1], 0)
 
 
 def on_device(
@@ -440,9 +444,9 @@
     dma = pltpu.SemaphoreType.DMA
     result = pl.pallas_call(
         kernel,
-        out_shape=jax.ShapeDtypeStruct((ROWS, D), jnp.bfloat16),
+        out_shape=pltpu.VMEM((ROWS, D), jnp.bfloat16),
         in_specs=[hbm, hbm, hbm, hbm, vmem, vmem, hbm, smem, smem],
-        out_specs=hbm,
+        out_specs=vmem,
         scratch_shapes=[
             pltpu.VMEM((ROWS, HD), jnp.bfloat16),
             pltpu.VMEM((3, 2, ROWS, HD), jnp.bfloat16),
@@ -453,7 +457,6 @@
             pltpu.VMEM((ROWS, D), jnp.float32),
             pltpu.VMEM((ROWS, D), jnp.bfloat16),
             dma((6,)),
-            dma((D // OUT_COLS,)),
             dma((HEADS,)),
             dma((HEADS,)),
             dma((HEADS,)),
@@ -468,7 +471,7 @@
             dma((30,)),
         ],
         compiler_params=pltpu.CompilerParams(
-            collective_id=0, has_side_effects=True, vmem_limit_bytes=60 * 2**20
+            collective_id=0, has_side_effects=True, vmem_limit_bytes=58 * 2**20
         ),
     )(
         queries[0],

time: 67.1 us -> 64 us (0.954)
  local copies, waits for them, and re-layouts: 3.76 us -> 1.67 us
  Pallas kernels: 63.2 us -> 62.2 us
    unnamed x1, local copies, waits for them, and re-layouts: 3.76 us -> 1.67 us
    pallas_call x1, Pallas kernels: 63.2 us -> 62.2 us  [on_device(): pl.pallas_call(kernel, out_shape=pltpu.VMEM((ROWS, D), jnp.bfloat16), in_...]
where the time goes in v3:
time: 64 us; the launch traced here: 63.8 us
  Pallas kernels  62.2 us (97%)
  local copies, waits for them, and re-layouts  1.67 us (3%)
    pallas_call x1, Pallas kernels, on_device(): pl.pallas_call(kernel, out_shape=pltpu.VMEM((ROWS, D), jnp.bfloat16), in_...  62.2 us
    unnamed x1, local copies, waits for them, and re-layouts  1.67 us

profile of v3, /device:TPU:1, one launch (start us, length us, event | category | flops | bytes accessed | tf_op | source)
XLA Modules:
  0.0 63.8 jit_solution(10430681147883725219)
XLA Ops:
  0.0 62.2 %shard_map.91 = bf16[512,3072]{1,0:T(8,128)(2,1)S(1)} custom-call(bf16[512,1536]{1,0:T(8,128)(2,1)} %bitcast.9, bf16[2,512,1536]{2,1,0:T(8,128)(2,1)} %bitcast.7, bf16[2,16,1536]{2,1,0:T(8,128)(2,1)} %bitcast.10, bf16[512,3072]{1,0:T(8,128)(2,1)} %bitcast.8, f32[1,3072]{1,0:T(1,128)} %gate.1, f32[1,3072]{1,0:T(1,128)} %bitcast.11, bf16[96,3072]{1,0:T(8,128)(2,1)} %w_hbm.1, ...), custom_call_target="tpu_custom_call" | custom-call | tf_op jit(solution)/shard_map/pallas_call | solution.py:445
  62.2 1.7 %copy.11 = bf16[1,512,3072]{2,1,0:T(8,128)(2,1)} copy(bf16[1,512,3072]{2,1,0:T(8,128)(2,1)S(1)} %bitcast.6) | data formatting | bytes 6291456

commit v4 on v3

--- a/solution.py
+++ b/solution.py
@@ -20,8 +20,8 @@
 SHARD = 96
 HALF = 48
 BLOCK = 256
-OUT_COLS = 512
-BLOCKS = 3
+OUT_COLS = 1536
+BLOCKS = 1
 SIDE = 768
 PART = 1536
 masked_score = -1e30
@@ -71,6 +71,38 @@
             total = part_total if i == 0 else total + part_total
             weighted = part_weighted if i == 0 else weighted + part_weighted
         att[pl.ds(start, BLOCK), col] = (weighted / total).astype(jnp.bfloat16)
+
+
+def attend_near(head, q, kvb, txt, mask):
+    col = columns_of(head)
+    states = []
+    for start in range(0, ROWS, BLOCK):
+        rows = q[pl.ds(start, BLOCK), col]
+        parts = [scores_of(rows, kvb[i, 0, :, col], start, mask, i) for i in range(2)]
+        parts.append(
+            lax.dot_general(rows, txt[0, :, col], CONTRACT_LAST, preferred_element_type=jnp.float32)
+        )
+        shift = largest_of(parts) * EXP2_SCALE
+        total, weighted = weigh(parts[2], shift, txt[1, :, col])
+        for i in range(2):
+            part_total, part_weighted = weigh(parts[i], shift, kvb[i, 1, :, col])
+            total, weighted = total + part_total, weighted + part_weighted
+        states.append((shift, total, weighted))
+    return states
+
+
+def attend_far(head, q, kvb, mask, att, states):
+    col = columns_of(head)
+    for start, (near_shift, total, weighted) in zip(range(0, ROWS, BLOCK), states):
+        rows = q[pl.ds(start, BLOCK), col]
+        scores = scores_of(rows, kvb[2, 0, :, col], start, mask, 2)
+        shift = jnp.maximum(near_shift, largest_of([scores]) * EXP2_SCALE)
+        scale = jnp.exp2(near_shift - shift)
+        far_total, far_weighted = weigh(scores, shift, kvb[2, 1, :, col])
+        total = total * scale + far_total
+        att[pl.ds(start, BLOCK), col] = ((weighted * scale + far_weighted) / total).astype(
+            jnp.bfloat16
+        )
 
 
 def kernel(
@@ -337,7 +369,6 @@
         8: [lambda: ring(1, 4)],
         9: [lambda: ring(2, 4), lambda: project_own(0)],
         10: [lambda: across(8)],
-        11: [lambda: project_own(1)],
     }
     own_side = pl.ds(pl.multiple_of(y_lo * SIDE, SIDE), SIDE)
     other_side = pl.ds(pl.multiple_of((1 - y_lo) * SIDE, SIDE), SIDE)
@@ -380,7 +411,17 @@
         attend_head(head, q, kvb, txt, mask, att)
         return 0
 
-    lax.fori_loop(0, HEADS, step, 0)
+    lax.fori_loop(0, HEADS - 1, step, 0)
+    last = head_of(HEADS - 1)
+    kv_near(last).wait_recv()
+    states = attend_near(last, q, kvb, txt, mask)
+    project_own(1)
+
+    @pl.when(has_far)
+    def _():
+        kv_far(last).wait_recv()
+
+    attend_far(last, q, kvb, mask, att, states)
 
     def finish(j, _):
         cols = pl.ds(pl.multiple_of(j * OUT_COLS, OUT_COLS), OUT_COLS)

time: 64 us -> 62.9 us (0.983)
  Pallas kernels: 62.2 us -> 61.1 us
    pallas_call x1, Pallas kernels: 62.2 us -> 61.1 us  [on_device(): pl.pallas_call(kernel, out_shape=pltpu.VMEM((ROWS, D), jnp.bfloat16), in_...]
where the time goes in v4:
time: 62.9 us; the launch traced here: 62.7 us
  Pallas kernels  61.1 us (97%)
  local copies, waits for them, and re-layouts  1.67 us (3%)
    pallas_call x1, Pallas kernels, on_device(): pl.pallas_call(kernel, out_shape=pltpu.VMEM((ROWS, D), jnp.bfloat16), in_...  61.1 us
    unnamed x1, local copies, waits for them, and re-layouts  1.67 us

profile of v4, /device:TPU:1, one launch (start us, length us, event | category | flops | bytes accessed | tf_op | source)
XLA Modules:
  0.0 62.7 jit_solution(14175091645798487715)
XLA Ops:
  0.0 61.1 %shard_map.91 = bf16[512,3072]{1,0:T(8,128)(2,1)S(1)} custom-call(bf16[512,1536]{1,0:T(8,128)(2,1)} %bitcast.9, bf16[2,512,1536]{2,1,0:T(8,128)(2,1)} %bitcast.7, bf16[2,16,1536]{2,1,0:T(8,128)(2,1)} %bitcast.10, bf16[512,3072]{1,0:T(8,128)(2,1)} %bitcast.8, f32[1,3072]{1,0:T(1,128)} %gate.1, f32[1,3072]{1,0:T(1,128)} %bitcast.11, bf16[96,3072]{1,0:T(8,128)(2,1)} %w_hbm.1, ...), custom_call_target="tpu_custom_call" | custom-call | tf_op jit(solution)/shard_map/pallas_call | solution.py:486
  61.1 1.7 %copy.11 = bf16[1,512,3072]{2,1,0:T(8,128)(2,1)} copy(bf16[1,512,3072]{2,1,0:T(8,128)(2,1)S(1)} %bitcast.6) | data formatting | bytes 6291456
